TPU v7x, 512 devices: a whole 4x8x8 slice. The times are simulated.
512 devices in a mesh: row: 16 (over x, y_hi, core), col: 32 (over y_lo, z).
Axes of the slice: x: 4, y: 8 (y_hi: 2, y_lo: 4; y = y_hi * 4 + y_lo), z: 8, core: 2. Of those that a mesh axis runs over, the one named last changes fastest.
Arguments:
- train_features: float32 [4096, 8192], P('col', 'row'), may hold values from -6 to 6
- inverse: float32 [8192, 8192], P('row', 'col'), may hold values from -0.0625 to 0.0625
- test_features: float32 [1024, 8192], P('row', 'col'), may hold values from -0.0625 to 0.0625
Outputs:
- scores: float32 [1024, 4096], P('col', 'row')
All inputs are finite; a program needn't handle non-finite values.
Results may differ from a plain program's by a relative error of at most 0.000071.
Values sent between devices are 32-bit elements; how exact they have to be, the bound alone decides.
A program may use at most 64 MiB of HBM per device.

v0:
```python
import jax
import jax.numpy as jnp
from jax import lax
from jax.sharding import PartitionSpec as P


def contract_last(left, right):
    return lax.dot_general(
        left,
        right,
        (((1,), (1,)), ((), ())),
        precision=lax.Precision.HIGHEST,
        preferred_element_type=jnp.float32,
    )


def on_device(train_features, inverse, test_features):
    test_block = lax.all_gather(test_features, "row", axis=0, tiled=True)
    partial_value = jnp.dot(
        lax.all_gather(train_features, "col", axis=0, tiled=True),
        inverse,
        precision=lax.Precision.HIGHEST,
        preferred_element_type=jnp.float32,
    )
    whitened = lax.psum_scatter(partial_value, "row", scatter_dimension=0, tiled=True)
    return lax.psum_scatter(
        contract_last(test_block, whitened), "col", scatter_dimension=0, tiled=True
    )


def solution(mesh):
    placed = (P("col", "row"), P("row", "col"), P("row", "col"))
    return jax.shard_map(
        on_device, mesh=mesh, in_specs=placed, out_specs=P("col", "row"), check_vma=False
    )
```

profile of v0, /device:TPU:4, one launch (start us, length us, event | category | flops | bytes accessed | tf_op | source)
XLA Modules:
  0.0 525.7 jit_solution(16660158069167475863)
XLA Ops:
  6.5 0.0 copy-start
  6.5 0.0 all-gather.3.cloned.1.call-start
  6.5 0.7 all-gather.3.cloned.1.call-update
  7.3 0.0 all-gather.5.cloned.1.call-start
  7.3 0.7 all-gather.5.cloned.1.call-update
  8.0 0.0 reduce-scatter.5.cloned.1.call-start
  8.1 176.3 %all-gather.3.cloned.1.call-done = f32[4096,512]{1,0:T(8,128)} async-done(((f32[128,512]{1,0:T(8,128)}), f32[4096,512]{1,0:T(8,128)}) %all-gather.3.cloned.1.call-update) | async-done | bytes 8388624 | tf_op jit(solution)/shard_map/all_gather | solution.py:20
  184.4 0.0 copy-done
  184.4 10.4 %fusion = f32[4096,256]{1,0:T(8,128)} fusion(f32[4096,512]{1,0:T(8,128)} %all-gather.3.cloned.1.call-done, f32[512,256]{1,0:T(8,128)S(1)} %copy-done), kind=kOutput, calls=%fused_computation.1 | convolution fusion | flops 6442450944 | bytes 13107200 | tf_op jit(solution)/shard_map/dot_general | solution.py:19
  194.8 0.0 reduce-scatter.5.cloned.1.call-update
  194.9 0.0 reduce-scatter.7.cloned.1.call-start
  194.9 46.9 %all-gather.5.cloned.1.call-done = f32[1024,256]{1,0:T(8,128)} async-done(((f32[64,256]{1,0:T(8,128)}), f32[1024,256]{1,0:T(8,128)}) %all-gather.5.cloned.1.call-update) | async-done | bytes 1048592 | tf_op jit(solution)/shard_map/all_gather | solution.py:18
  241.8 113.3 %reduce-scatter.5.cloned.1.call-done = f32[256,256]{1,0:T(8,128)} async-done(((f32[4096,256]{1,0:T(8,128)}), f32[256,256]{1,0:T(8,128)}) %reduce-scatter.5.cloned.1.call-update) | async-done | bytes 262160 | tf_op jit(solution)/shard_map/reduce_scatter | solution.py:25
  355.1 2.4 convolution_bitcast_fusion
  357.5 1.3 copy.6
  358.8 0.0 reduce-scatter.7.cloned.1.call-update
  358.8 160.3 %reduce-scatter.7.cloned.1.call-done = f32[32,256]{1,0:T(8,128)} async-done(((f32[1024,256]{1,0:T(8,128)}), f32[32,256]{1,0:T(8,128)}) %reduce-scatter.7.cloned.1.call-update) | async-done | bytes 32784 | tf_op jit(solution)/shard_map/reduce_scatter | solution.py:26
Async XLA Ops:
  6.5 177.8 %copy-start = (f32[512,256]{1,0:T(8,128)S(1)}, f32[512,256]{1,0:T(8,128)}, u32[]{:S(2)}) copy-start(f32[512,256]{1,0:T(8,128)} %param.4) | copy-start | bytes 1572868
  6.5 177.8 %all-gather.3.cloned.1.call-start = ((), (), s32[]{:S(2)}) async-start(), calls=%async_computation.2 | async-start | bytes 8650752 | tf_op jit(solution)/shard_map/all_gather | solution.py:20
  7.3 234.6 %all-gather.5.cloned.1.call-start = ((), (), s32[]{:S(2)}) async-start(), calls=%async_computation.4 | async-start | bytes 1114112 | tf_op jit(solution)/shard_map/all_gather | solution.py:18
  8.0 347.1 %reduce-scatter.5.cloned.1.call-start = ((), (), s32[]{:S(2)}) async-start(), calls=%async_computation.3 | async-start | bytes 4456448 | tf_op jit(solution)/shard_map/reduce_scatter | solution.py:25
  194.9 324.3 %reduce-scatter.7.cloned.1.call-start = ((), (), s32[]{:S(2)}) async-start(), calls=%async_computation.5 | async-start | bytes 1081344 | tf_op jit(solution)/shard_map/reduce_scatter | solution.py:26
Sparse Core Ops, SparseCore 0:
  9.4 174.8 all-gather.2
  187.6 54.1 all-gather.4
  246.8 108.3 reduce-scatter.4
  358.9 160.1 reduce-scatter.6
where the time goes:
time: 526 us
  waiting for transfers between devices  498 us (95%)
  between operations  13.1 us (2%)
  matrix products  12.8 us (2%)
    all_gather x1, waiting for transfers between devices, on_device(): lax.all_gather(train_features, 'col', axis=0, tiled=True)  176 us
    reduce_scatter x1, waiting for transfers between devices, on_device(): lax.psum_scatter(contract_last(test_block, whitened), 'col', scatter_dime...  160 us
    reduce_scatter x1, waiting for transfers between devices, on_device(): lax.psum_scatter(partial_value, 'row', scatter_dimension=0, tiled=True)  113 us
    all_gather x1, waiting for transfers between devices, on_device(): test_block = lax.all_gather(test_features, 'row', axis=0, tiled=True)  46.9 us
  transfers between devices with their start and end apart: 4, of which 4 were waited for; matrix products, arithmetic and copies ran while one was open for 2% of the time, Pallas kernels for 0%

commit v1 on v0

v1 whole, which is shorter than its diff:
```python
import functools

import jax
import jax.numpy as jnp
from jax import lax
from jax.experimental import pallas as pl
from jax.experimental.pallas import tpu as pltpu
from jax.sharding import PartitionSpec as P

MESH = pl.DeviceIdType.MESH
F32 = jnp.float32
BF16 = jnp.bfloat16


def split(value):
    high = value.astype(BF16)
    return high, (value - high.astype(F32)).astype(BF16)


def dot_nt(left, right):
    def product(a, b):
        return lax.dot_general(a, b, (((1,), (1,)), ((), ())), preferred_element_type=F32)

    return product(left[0], right[1]) + product(left[1], right[0]) + product(left[0], right[0])


def device(x, yh, core, yl, z):
    return ((x * 2 + yh) * 2 + core, yl * 8 + z)


def kernel(
    x_ref, m_ref, t_ref, o_ref,
    mb, xb, ty, tb, u, rs, ag, op, fr,
    local_sem, m_send, m_recv, x_send, x_recv, ty_send, ty_recv, t_send, t_recv,
    rs_send, rs_recv, ag_send, ag_recv, f_send, f_recv,
):
    r = lax.axis_index("row")
    c = lax.axis_index("col")
    k = r % 2
    yh = (r // 2) % 2
    x = r // 4
    rp = r // 2
    yl = c // 8
    z = c % 8
    p = z % 2
    w = z // 2

    def remote(src, dst, send, recv, to):
        return pltpu.make_async_remote_copy(
            src_ref=src, dst_ref=dst, send_sem=send, recv_sem=recv, device_id=to, device_id_type=MESH
        )

    sibling = device(x, yh, 1 - k, yl, z)
    across = device(x, 1 - yh, k, yl, z)
    partner = device(x, yh, k, yl, z + 1 - 2 * p)

    def along_x(dx, dp):
        zz = z if dp == 0 else z + 1 - 2 * p
        return device((x + dx) % 4, yh, k, yl, zz)

    def along_col(dy, dw):
        return device(x, yh, k, (yl + dy) % 4, 2 * ((w + dw) % 4) + p)

    barrier = pltpu.get_barrier_semaphore()
    greeted = [across, sibling]
    greeted += [along_x(dx, dp) for dx in range(4) for dp in range(2) if dx or dp]
    greeted += [along_col(dy, dw) for dy in range(4) for dw in range(4) if dy or dw]
    for to in greeted:
        pl.semaphore_signal(barrier, inc=1, device_id=to, device_id_type=MESH)

    own_m = pltpu.make_async_copy(m_ref, mb.at[0, 0], local_sem.at[0])
    own_x = pltpu.make_async_copy(x_ref, xb.at[0, 0], local_sem.at[1])
    own_t = pltpu.make_async_copy(
        t_ref.at[pl.ds(pl.multiple_of(32 * p, 32), 32)],
        tb.at[0, pl.ds(pl.multiple_of(32 * rp, 32), 32)],
        local_sem.at[2],
    )
    own_m.start()
    own_x.start()
    own_t.start()

    pl.semaphore_wait(barrier, len(greeted))

    copy_ty = remote(t_ref, ty, ty_send, ty_recv, across)
    copy_ty.start()
    t_copies = []

    def send_t(block_ref, b):
        rows = pl.ds(pl.multiple_of(32 * (2 * x + (yh if b == 0 else 1 - yh)), 32), 32)
        for dx in (2, 1, 3, 0):
            for dp in range(2):
                if dx == 0 and dp == 0:
                    continue
                half = p if dp == 0 else 1 - p
                n = (b * 4 + dx) * 2 + dp
                copy = remote(
                    block_ref.at[pl.ds(pl.multiple_of(32 * half, 32), 32)],
                    tb.at[dp, rows], t_send.at[n], t_recv.at[n], along_x(dx, dp),
                )
                copy.start()
                t_copies.append(copy)

    send_t(t_ref, 0)
    copy_mp = remote(m_ref, mb.at[1, 0], m_send.at[0], m_recv.at[0], partner)
    copy_mp.start()
    copy_ms = remote(m_ref, mb.at[0, 1], m_send.at[1], m_recv.at[1], sibling)
    copy_ms.start()
    copy_ty.wait_recv()
    send_t(ty, 1)
    own_ty = pltpu.make_async_copy(
        ty.at[pl.ds(pl.multiple_of(32 * p, 32), 32)],
        tb.at[0, pl.ds(pl.multiple_of(32 * (2 * x + 1 - yh), 32), 32)],
        local_sem.at[3],
    )
    own_ty.start()

    x_copies = []
    for d in (1, 2, 3):
        to = device(x, yh, k, (yl + d) % 4, z)
        copy = remote(x_ref, xb.at[4 - d, 0], x_send.at[4 - d], x_recv.at[4 - d], to)
        copy.start()
        x_copies.append(copy)
    copy_xs = remote(x_ref, xb.at[0, 1], x_send.at[4], x_recv.at[4], sibling)
    copy_xs.start()

    own_m.wait()
    own_t.wait()
    own_ty.wait()
    for copy in t_copies:
        copy.wait_recv()
    copy_mp.wait_recv()
    copy_mr = remote(mb.at[1, 0], mb.at[1, 1], m_send.at[2], m_recv.at[2], sibling)
    copy_mr.start()

    t_halves = [split(tb[q]) for q in range(2)]
    rs_copies = [[], []]
    for cr in range(2):
        if cr == 1:
            copy_ms.wait_recv()
            copy_mr.wait_recv()
        u[cr] = dot_nt(t_halves[0], split(mb[0, cr])) + dot_nt(t_halves[1], split(mb[1, cr]))
        for dw in (2, 1, 3, 0):
            for dy in (2, 1, 3, 0):
                e = dy * 4 + dw
                if e == 0:
                    continue
                m = 4 * ((yl + dy) % 4) + (w + dw) % 4
                copy = remote(
                    u.at[cr, pl.ds(pl.multiple_of(16 * m, 16), 16)], rs.at[cr, e],
                    rs_send.at[cr, e], rs_recv.at[cr, e], along_col(dy, dw),
                )
                copy.start()
                rs_copies[cr].append(copy)

    mine = pl.ds(pl.multiple_of(16 * (4 * yl + w), 16), 16)
    slot = (z // 4) * 4 + (z % 2) * 2 + (z // 2) % 2
    slot_rows = pl.ds(pl.multiple_of(16 * slot, 16), 16)
    ag_copies = [[], []]
    for cr in range(2):
        for copy in rs_copies[cr]:
            copy.wait_recv()
        total = u[cr, mine]
        for e in range(1, 16):
            total = total + rs[cr, e]
        ag[cr, slot_rows] = total
        for dz in (4, 3, 5, 2, 6, 1, 7):
            to = device(x, yh, k, yl, (z + dz) % 8)
            copy = remote(
                ag.at[cr, slot_rows], ag.at[cr, slot_rows], ag_send.at[cr, dz], ag_recv.at[cr, dz], to
            )
            copy.start()
            ag_copies[cr].append(copy)
        if cr == 0:
            own_x.wait()
            relays = []
            for copy, d in zip(x_copies, (3, 2, 1)):
                copy.wait_recv()
                relay = remote(xb.at[d, 0], xb.at[d, 1], x_send.at[4 + d], x_recv.at[4 + d], sibling)
                relay.start()
                relays.append(relay)
            copy_xs.wait_recv()
            for relay in relays:
                relay.wait_recv()

    for cr in range(2):
        for copy in ag_copies[cr]:
            copy.wait_recv()
    a = [split(ag[cr]) for cr in range(2)]

    def same(to):
        return jnp.logical_and(to[0] == r, to[1] == c)

    finals = []
    for d in range(4):
        op[d] = dot_nt(a[0], split(xb[d, 0])) + dot_nt(a[1], split(xb[d, 1]))
        for g in range(2):
            for q in range(2):
                n = (d * 2 + g) * 2 + q
                to = device((yl + d) % 4, z // 4, (z // 2) % 2, yl, 4 * g + 2 * k + q)
                rows = pl.ds(32 * (2 * g + q), 32)
                here = same(to)
                copy = remote(
                    op.at[d, rows], fr.at[rp, z % 2], f_send.at[n], f_recv.at[rp, z % 2], to
                )
                finals.append((here, copy))

                @pl.when(jnp.logical_not(here))
                def _(copy=copy):
                    copy.start()

                @pl.when(here)
                def _(d=d, rows=rows):
                    fr[rp, z % 2] = op[d, rows]

    for half in range(2):
        total = None
        for s in range(8):
            z_from = 4 * yh + 2 * k + half
            here = jnp.logical_and(
                jnp.logical_and(rp == s, z_from == z), k == (z // 2) % 2
            )
            arrival = remote(
                op.at[0, pl.ds(0, 32)], fr.at[s, half], f_send.at[0], f_recv.at[s, half], sibling
            )

            @pl.when(jnp.logical_not(here))
            def _(arrival=arrival):
                arrival.wait_recv()

        total = fr[0, half]
        for s in range(1, 8):
            total = total + fr[s, half]
        o_ref[:, pl.ds(128 * half, 128)] = total

    copy_ty.wait_send()
    for copy in t_copies + x_copies + relays + rs_copies[0] + rs_copies[1] + ag_copies[0] + ag_copies[1]:
        copy.wait_send()
    for copy in (copy_mp, copy_ms, copy_mr, copy_xs):
        copy.wait_send()
    for here, copy in finals:

        @pl.when(jnp.logical_not(here))
        def _(copy=copy):
            copy.wait_send()


def on_device(train_features, inverse, test_features):
    vmem = pltpu.VMEM
    dma = pltpu.SemaphoreType.DMA
    return pl.pallas_call(
        kernel,
        out_shape=jax.ShapeDtypeStruct((32, 256), F32),
        in_specs=[pl.BlockSpec(memory_space=pl.ANY)] * 3,
        out_specs=pl.BlockSpec(memory_space=pltpu.VMEM),
        scratch_shapes=[
            vmem((2, 2, 512, 256), F32),
            vmem((4, 2, 128, 512), F32),
            vmem((64, 256), F32),
            vmem((2, 256, 256), F32),
            vmem((2, 256, 512), F32),
            vmem((2, 16, 16, 512), F32),
            vmem((2, 128, 512), F32),
            vmem((4, 128, 128), F32),
            vmem((8, 2, 32, 128), F32),
            dma((4,)),
            dma((3,)), dma((3,)),
            dma((8,)), dma((8,)),
            dma, dma,
            dma((16,)), dma((16,)),
            dma((2, 16)), dma((2, 16)),
            dma((2, 8)), dma((2, 8)),
            dma((16,)), dma((8, 2)),
        ],
        compiler_params=pltpu.CompilerParams(
            collective_id=0, has_side_effects=True, vmem_limit_bytes=48 * 2**20
        ),
        cost_estimate=pl.CostEstimate(flops=2 * 3 * 402653184 // 2, bytes_accessed=2 * 2**20, transcendentals=0),
        name="scores",
    )(train_features, inverse, test_features)


def solution(mesh):
    placed = (P("col", "row"), P("row", "col"), P("row", "col"))
    return jax.shard_map(
        on_device, mesh=mesh, in_specs=placed, out_specs=P("col", "row"), check_vma=False
    )
```

time: 526 us -> 98.7 us (0.19)
  the two profiles are of different devices: /device:TPU:4 before, /device:TPU:9 now
where the time goes in v1:
time: 98.7 us; the launch traced here: 98.5 us
  Pallas kernels  95 us (96%)
  local copies, waits for them, and re-layouts  3.45 us (3%)
    pallas_call x1, Pallas kernels, on_device(): pl.pallas_call(kernel, out_shape=jax.ShapeDtypeStruct((32, 256), F32), in...  95 us
    unnamed x7, local copies, waits for them, and re-layouts  3.45 us

profile of v1, /device:TPU:9, one launch (start us, length us, event | category | flops | bytes accessed | tf_op | source)
XLA Modules:
  0.0 98.5 jit_solution(9656787242771020748)
XLA Ops:
  0.0 0.0 copy-start
  0.0 1.0 %copy-done = f32[512,256]{1,0:T(8,128)S(1)} copy-done((f32[512,256]{1,0:T(8,128)S(1)}, f32[512,256]{1,0:T(8,128)}, u32[]{:S(2)}) %copy-start) | copy-done | bytes 524312
  1.0 0.0 copy-start.1
  1.0 0.9 copy-done.1
  2.0 0.0 copy-start.2
  2.0 0.8 copy-done.2
  2.8 95.0 %scores.1 = f32[32,256]{1,0:T(8,128)S(1)} custom-call(f32[128,512]{1,0:T(8,128)S(1)} %copy-done.1, f32[512,256]{1,0:T(8,128)S(1)} %copy-done, f32[64,256]{1,0:T(8,128)S(1)} %copy-done.2), custom_call_target="tpu_custom_call" | custom-call | flops 1207959552 | bytes 2097152 | tf_op jit(solution)/shard_map/scores/pallas_call | solution.py:250
  97.9 0.6 copy.5
Async XLA Ops:
  0.0 1.0 %copy-start = (f32[512,256]{1,0:T(8,128)S(1)}, f32[512,256]{1,0:T(8,128)}, u32[]{:S(2)}) copy-start(f32[512,256]{1,0:T(8,128)} %m_ref.1) | copy-start | bytes 1572868
  1.0 0.9 copy-start.1
  2.0 0.8 copy-start.2

commit v2 on v1

v2 whole, which is shorter than its diff:
```python
import jax
import jax.numpy as jnp
from jax import lax
from jax.experimental import pallas as pl
from jax.experimental.pallas import tpu as pltpu
from jax.sharding import PartitionSpec as P

MESH = pl.DeviceIdType.MESH
F32 = jnp.float32
BF16 = jnp.bfloat16
CHUNKS = ((0, 0), (0, 1), (1, 0), (1, 1))


def split(value):
    high = value.astype(BF16)
    return high, (value - high.astype(F32)).astype(BF16)


def dot_nt(left, right):
    def product(a, b):
        return lax.dot_general(a, b, (((1,), (1,)), ((), ())), preferred_element_type=F32)

    return product(left[0], right[1]) + product(left[1], right[0]) + product(left[0], right[0])


def device(x, yh, core, yl, z):
    return ((x * 2 + yh) * 2 + core, yl * 8 + z)


def kernel(
    x_ref, m_ref, t_ref, o_ref,
    mb, xb, ty, tb, u, rs, ag, op, fr,
    local_sem, m_send, m_recv, x_send, x_recv, ty_send, ty_recv, t_send, t_recv,
    rs_send, rs_recv, ag_send, ag_recv, f_send, f_recv,
):
    r = lax.axis_index("row")
    c = lax.axis_index("col")
    k = r % 2
    yh = (r // 2) % 2
    x = r // 4
    rp = r // 2
    yl = c // 8
    z = c % 8
    p = z % 2
    w = z // 2
    step = (1 - 2 * p) * (1 - 2 * k)

    def remote(src, dst, send, recv, to):
        return pltpu.make_async_remote_copy(
            src_ref=src, dst_ref=dst, send_sem=send, recv_sem=recv, device_id=to, device_id_type=MESH
        )

    def rows(start, size):
        return pl.ds(pl.multiple_of(start, size), size)

    sibling = device(x, yh, 1 - k, yl, z)
    across = device(x, 1 - yh, k, yl, z)

    def along_x(dx, q):
        zz = (z, (z + step) % 8, (z - step) % 8)[q]
        return device((x + dx) % 4, yh, k, yl, zz)

    def along_col(dy, dw):
        return device(x, yh, k, (yl + dy) % 4, 2 * ((w + dw) % 4) + p)

    barrier = pltpu.get_barrier_semaphore()
    greeted = [across, sibling]
    greeted += [along_x(dx, q) for dx in range(4) for q in range(3) if dx or q]
    greeted += [along_col(dy, dw) for dy in range(4) for dw in range(4) if dy or dw]
    for to in greeted:
        pl.semaphore_signal(barrier, inc=1, device_id=to, device_id_type=MESH)

    own_m = pltpu.make_async_copy(m_ref, mb.at[0, 0], local_sem.at[0])
    own_x = pltpu.make_async_copy(x_ref, xb.at[0, 0], local_sem.at[1])
    own_t = pltpu.make_async_copy(t_ref.at[rows(4 * p, 4)], tb.at[0, rows(4 * rp, 4)], local_sem.at[2])
    own_m.start()
    own_x.start()
    own_t.start()

    pl.semaphore_wait(barrier, len(greeted))

    copy_ty = remote(t_ref, ty, ty_send, ty_recv, across)
    copy_ty.start()
    t_copies = [[], [], []]

    def send_t(block_ref, b):
        to_rows = rows(4 * (2 * x + (yh if b == 0 else 1 - yh)), 4)
        for dx in (2, 1, 3, 0):
            for q in (1, 0, 2):
                if dx == 0 and q == 0:
                    continue
                half = p if q == 0 else 1 - p
                n = (b * 4 + dx) * 3 + q
                copy = remote(
                    block_ref.at[rows(4 * half, 4)], tb.at[q, to_rows],
                    t_send.at[n], t_recv.at[n], along_x(dx, q),
                )
                copy.start()
                t_copies[q].append(copy)

    send_t(t_ref, 0)
    copy_mp = remote(m_ref, mb.at[1, 0], m_send.at[0], m_recv.at[0], along_x(0, 1))
    copy_mp.start()
    copy_ms = remote(m_ref, mb.at[0, 1], m_send.at[1], m_recv.at[1], sibling)
    copy_ms.start()
    copy_ty.wait_recv()
    send_t(ty, 1)
    own_ty = pltpu.make_async_copy(
        ty.at[rows(4 * p, 4)], tb.at[0, rows(4 * (2 * x + 1 - yh), 4)], local_sem.at[3]
    )
    own_ty.start()

    x_copies = {}

    def send_x(d):
        to = device(x, yh, k, (yl + d) % 4, z)
        copy = remote(x_ref, xb.at[4 - d, 0], x_send.at[4 - d], x_recv.at[4 - d], to)
        copy.start()
        x_copies[4 - d] = copy

    send_x(1)
    send_x(3)
    copy_xs = remote(x_ref, xb.at[0, 1], x_send.at[4], x_recv.at[4], sibling)
    copy_xs.start()

    own_m.wait()
    own_t.wait()
    own_ty.wait()
    for copy in t_copies[0] + t_copies[1]:
        copy.wait_recv()
    copy_mp.wait_recv()
    copy_mr = remote(mb.at[1, 0], mb.at[1, 1], m_send.at[2], m_recv.at[2], sibling)
    copy_mr.start()

    rs_copies = []
    for ch, (tc, ic) in enumerate(CHUNKS):
        if ch == 1:
            for copy in t_copies[2]:
                copy.wait_recv()
            copy_ms.wait_recv()
            copy_mr.wait_recv()

        def test_rows(q):
            return split(tb[q].reshape(8, 2, 16, 256)[:, tc].reshape(128, 256))

        u[ch] = dot_nt(test_rows(0), split(mb[0, ic])) + dot_nt(test_rows(1 + ic), split(mb[1, ic]))
        copies = []
        for dw in (2, 1, 3, 0):
            for dy in (2, 1, 3, 0):
                e = dy * 4 + dw
                if e == 0:
                    continue
                m = 4 * ((yl + dy) % 4) + (w + dw) % 4
                copy = remote(
                    u.at[ch, rows(8 * m, 8)], rs.at[ch, e],
                    rs_send.at[ch, e], rs_recv.at[ch, e], along_col(dy, dw),
                )
                copy.start()
                copies.append(copy)
        rs_copies.append(copies)
        if ch == 1:
            send_x(2)

    mine = rows(8 * (4 * yl + w), 8)
    slot = (z // 4) * 4 + (z % 2) * 2 + (z // 2) % 2
    slot_rows = rows(8 * slot, 8)
    ag_copies = []
    relays = []
    for ch in range(4):
        for copy in rs_copies[ch]:
            copy.wait_recv()
        total = u[ch, mine]
        for e in range(1, 16):
            total = total + rs[ch, e]
        ag[ch, slot_rows] = total
        copies = []
        for dz in (4, 3, 5, 2, 6, 1, 7):
            to = device(x, yh, k, yl, (z + dz) % 8)
            copy = remote(
                ag.at[ch, slot_rows], ag.at[ch, slot_rows], ag_send.at[ch, dz], ag_recv.at[ch, dz], to
            )
            copy.start()
            copies.append(copy)
        ag_copies.append(copies)
        for d in ((), (1, 3), (2,), ())[ch]:
            x_copies[d].wait_recv()
            relay = remote(xb.at[d, 0], xb.at[d, 1], x_send.at[4 + d], x_recv.at[4 + d], sibling)
            relay.start()
            relays.append(relay)

    own_x.wait()
    copy_xs.wait_recv()
    for relay in relays:
        relay.wait_recv()

    finals = []
    for tc in range(2):
        for ch in (2 * tc, 2 * tc + 1):
            for copy in ag_copies[ch]:
                copy.wait_recv()
        a = [split(ag[2 * tc + ic]) for ic in range(2)]
        for d in range(4):
            op[tc, d] = dot_nt(a[0], split(xb[d, 0])) + dot_nt(a[1], split(xb[d, 1]))
            for g in range(2):
                for q in range(2):
                    n = ((tc * 4 + d) * 2 + g) * 2 + q
                    to = device((yl + d) % 4, z // 4, (z // 2) % 2, yl, 4 * g + 2 * k + q)
                    here = jnp.logical_and(to[0] == r, to[1] == c)
                    tile = pl.ds(16 * (2 * g + q), 16)
                    place = pl.ds(16 * tc, 16)
                    copy = remote(
                        op.at[tc, d, tile], fr.at[rp, z % 2, place],
                        f_send.at[n], f_recv.at[tc, rp, z % 2], to,
                    )
                    finals.append((here, copy))

                    @pl.when(jnp.logical_not(here))
                    def _(copy=copy):
                        copy.start()

                    @pl.when(here)
                    def _(d=d, tile=tile, place=place):
                        fr[rp, z % 2, place] = op[tc, d, tile]

    for tc in range(2):
        place = pl.ds(16 * tc, 16)
        for half in range(2):
            for s in range(8):
                z_from = 4 * yh + 2 * k + half
                here = jnp.logical_and(
                    jnp.logical_and(rp == s, z_from == z), k == (z // 2) % 2
                )
                arrival = remote(
                    op.at[0, 0, pl.ds(0, 16)], fr.at[s, half, place],
                    f_send.at[0], f_recv.at[tc, s, half], sibling,
                )

                @pl.when(jnp.logical_not(here))
                def _(arrival=arrival):
                    arrival.wait_recv()

            total = fr[0, half, place]
            for s in range(1, 8):
                total = total + fr[s, half, place]
            o_ref[place, pl.ds(128 * half, 128)] = total

    copy_ty.wait_send()
    for copies in t_copies + rs_copies + ag_copies + [relays, list(x_copies.values())]:
        for copy in copies:
            copy.wait_send()
    for copy in (copy_mp, copy_ms, copy_mr, copy_xs):
        copy.wait_send()
    for here, copy in finals:

        @pl.when(jnp.logical_not(here))
        def _(copy=copy):
            copy.wait_send()


def on_device(train_features, inverse, test_features):
    vmem = pltpu.VMEM
    dma = pltpu.SemaphoreType.DMA
    return pl.pallas_call(
        kernel,
        out_shape=jax.ShapeDtypeStruct((32, 256), F32),
        in_specs=[pl.BlockSpec(memory_space=pltpu.HBM)] * 3,
        out_specs=pl.BlockSpec(memory_space=pltpu.VMEM),
        scratch_shapes=[
            vmem((2, 2, 512, 256), F32),
            vmem((4, 2, 128, 512), F32),
            vmem((8, 8, 256), F32),
            vmem((3, 32, 8, 256), F32),
            vmem((4, 128, 512), F32),
            vmem((4, 16, 8, 512), F32),
            vmem((4, 64, 512), F32),
            vmem((2, 4, 64, 128), F32),
            vmem((8, 2, 32, 128), F32),
            dma((4,)),
            dma((3,)), dma((3,)),
            dma((8,)), dma((8,)),
            dma, dma,
            dma((24,)), dma((24,)),
            dma((4, 16)), dma((4, 16)),
            dma((4, 8)), dma((4, 8)),
            dma((32,)), dma((2, 8, 2)),
        ],
        compiler_params=pltpu.CompilerParams(
            collective_id=0, has_side_effects=True, vmem_limit_bytes=48 * 2**20
        ),
        cost_estimate=pl.CostEstimate(flops=1207959552, bytes_accessed=2 * 2**20, transcendentals=0),
        name="scores",
    )(train_features, inverse, test_features.reshape(8, 8, 256))


def solution(mesh):
    placed = (P("col", "row"), P("row", "col"), P("row", "col"))
    return jax.shard_map(
        on_device, mesh=mesh, in_specs=placed, out_specs=P("col", "row"), check_vma=False
    )
```

time: 98.7 us -> 94.2 us (0.954)
  the two profiles are of different devices: /device:TPU:9 before, /device:TPU:33 now
where the time goes in v2:
time: 94.2 us; the launch traced here: 94 us
  Pallas kernels  90.6 us (96%)
  local copies, waits for them, and re-layouts  3.45 us (4%)
    pallas_call x1, Pallas kernels, on_device(): pl.pallas_call(kernel, out_shape=jax.ShapeDtypeStruct((32, 256), F32), in...  90.6 us
    unnamed x7, local copies, waits for them, and re-layouts  3.45 us

profile of v2, /device:TPU:33, one launch (start us, length us, event | category | flops | bytes accessed | tf_op | source)
XLA Modules:
  0.0 94.0 jit_solution(14752966308478121271)
XLA Ops:
  0.0 0.0 copy-start
  0.0 1.0 %copy-done = f32[512,256]{1,0:T(8,128)S(1)} copy-done((f32[512,256]{1,0:T(8,128)S(1)}, f32[512,256]{1,0:T(8,128)}, u32[]{:S(2)}) %copy-start) | copy-done | bytes 524312
  1.0 0.0 copy-start.1
  1.0 0.9 %copy-done.1 = f32[128,512]{1,0:T(8,128)S(1)} copy-done((f32[128,512]{1,0:T(8,128)S(1)}, f32[128,512]{1,0:T(8,128)}, u32[]{:S(2)}) %copy-start.1) | copy-done | bytes 262168
  2.0 0.0 copy-start.2
  2.0 0.8 copy-done.2
  2.8 90.6 %scores.1 = f32[32,256]{1,0:T(8,128)S(1)} custom-call(f32[128,512]{1,0:T(8,128)S(1)} %copy-done.1, f32[512,256]{1,0:T(8,128)S(1)} %copy-done, f32[8,8,256]{2,1,0:T(8,128)S(1)} %bitcast.1), custom_call_target="tpu_custom_call" | custom-call | flops 1207959552 | bytes 2097152 | tf_op jit(solution)/shard_map/scores/pallas_call | solution.py:263
  93.4 0.6 copy.5
Async XLA Ops:
  0.0 1.0 %copy-start = (f32[512,256]{1,0:T(8,128)S(1)}, f32[512,256]{1,0:T(8,128)}, u32[]{:S(2)}) copy-start(f32[512,256]{1,0:T(8,128)} %m_ref.1) | copy-start | bytes 1572868
  1.0 0.9 %copy-start.1 = (f32[128,512]{1,0:T(8,128)S(1)}, f32[128,512]{1,0:T(8,128)}, u32[]{:S(2)}) copy-start(f32[128,512]{1,0:T(8,128)} %x_ref.1) | copy-start | bytes 786436
  2.0 0.8 copy-start.2

commit v3 on v2

--- a/solution.py
+++ b/solution.py
@@ -29,9 +29,9 @@
 
 def kernel(
     x_ref, m_ref, t_ref, o_ref,
-    mb, xb, ty, tb, u, rs, ag, op, fr,
+    mb, xb, ty, tb, u, ra, sb, rb, ag, op, fr,
     local_sem, m_send, m_recv, x_send, x_recv, ty_send, ty_recv, t_send, t_recv,
-    rs_send, rs_recv, ag_send, ag_recv, f_send, f_recv,
+    ra_send, ra_recv, rb_send, rb_recv, ag_send, ag_recv, f_send, f_recv,
 ):
     r = lax.axis_index("row")
     c = lax.axis_index("col")
@@ -60,18 +60,21 @@
         zz = (z, (z + step) % 8, (z - step) % 8)[q]
         return device((x + dx) % 4, yh, k, yl, zz)
 
-    def along_col(dy, dw):
-        return device(x, yh, k, (yl + dy) % 4, 2 * ((w + dw) % 4) + p)
+    def along_y(d):
+        return device(x, yh, k, (yl + d) % 4, z)
+
+    def along_z(d):
+        return device(x, yh, k, yl, 2 * ((w + d) % 4) + p)
 
     barrier = pltpu.get_barrier_semaphore()
     greeted = [across, sibling]
     greeted += [along_x(dx, q) for dx in range(4) for q in range(3) if dx or q]
-    greeted += [along_col(dy, dw) for dy in range(4) for dw in range(4) if dy or dw]
+    greeted += [along_y(d) for d in (1, 2, 3)] + [along_z(d) for d in (1, 2, 3)]
     for to in greeted:
         pl.semaphore_signal(barrier, inc=1, device_id=to, device_id_type=MESH)
 
     own_m = pltpu.make_async_copy(m_ref, mb.at[0, 0], local_sem.at[0])
-    own_x = pltpu.make_async_copy(x_ref, xb.at[0, 0], local_sem.at[1])
+    own_x = pltpu.make_async_copy(x_ref, xb.at[yl, 0], local_sem.at[1])
     own_t = pltpu.make_async_copy(t_ref.at[rows(4 * p, 4)], tb.at[0, rows(4 * rp, 4)], local_sem.at[2])
     own_m.start()
     own_x.start()
@@ -110,17 +113,41 @@
     )
     own_ty.start()
 
-    x_copies = {}
-
-    def send_x(d):
-        to = device(x, yh, k, (yl + d) % 4, z)
-        copy = remote(x_ref, xb.at[4 - d, 0], x_send.at[4 - d], x_recv.at[4 - d], to)
-        copy.start()
-        x_copies[4 - d] = copy
+    x_hops = []
+
+    def send_x(hop):
+        for way, side in enumerate((1, -1)):
+            block = yl - side * (hop - 1)
+            there = yl + side
+            n = 3 * way + hop - 1
+            sends = jnp.logical_and(
+                jnp.logical_and(block >= 0, block <= 3), jnp.logical_and(there >= 0, there <= 3)
+            )
+            comes = yl - side * hop
+            receives = jnp.logical_and(comes >= 0, comes <= 3)
+            source = x_ref if hop == 1 else xb.at[jnp.clip(block, 0, 3), 0]
+            copy = remote(
+                source, xb.at[jnp.clip(block, 0, 3), 0], x_send.at[n], x_recv.at[n],
+                device(x, yh, k, (yl + side) % 4, z),
+            )
+            slot = jnp.clip(comes, 0, 3)
+            relay = remote(xb.at[slot, 0], xb.at[slot, 1], x_send.at[7 + n], x_recv.at[7 + n], sibling)
+            x_hops.append((sends, receives, copy, relay))
+
+            @pl.when(sends)
+            def _(copy=copy):
+                copy.start()
+
+    def pass_x(hop):
+        for sends, receives, copy, relay in x_hops[2 * hop - 2:2 * hop]:
+
+            @pl.when(receives)
+            def _(copy=copy, relay=relay):
+                copy.wait_recv()
+                relay.start()
 
     send_x(1)
-    send_x(3)
-    copy_xs = remote(x_ref, xb.at[0, 1], x_send.at[4], x_recv.at[4], sibling)
+    copy_xs = remote(x_ref, xb.at[yl, 1], x_send.at[6], x_recv.at[6], sibling)
     copy_xs.start()
 
     own_m.wait()
@@ -132,7 +159,7 @@
     copy_mr = remote(mb.at[1, 0], mb.at[1, 1], m_send.at[2], m_recv.at[2], sibling)
     copy_mr.start()
 
-    rs_copies = []
+    ra_copies = []
     for ch, (tc, ic) in enumerate(CHUNKS):
         if ch == 1:
             for copy in t_copies[2]:
@@ -143,36 +170,51 @@
         def test_rows(q):
             return split(tb[q].reshape(8, 2, 16, 256)[:, tc].reshape(128, 256))
 
-        u[ch] = dot_nt(test_rows(0), split(mb[0, ic])) + dot_nt(test_rows(1 + ic), split(mb[1, ic]))
+        u[ch] = (
+            dot_nt(test_rows(0), split(mb[0, ic])) + dot_nt(test_rows(1 + ic), split(mb[1, ic]))
+        ).reshape(4, 4, 8, 512)
         copies = []
-        for dw in (2, 1, 3, 0):
-            for dy in (2, 1, 3, 0):
-                e = dy * 4 + dw
-                if e == 0:
-                    continue
-                m = 4 * ((yl + dy) % 4) + (w + dw) % 4
-                copy = remote(
-                    u.at[ch, rows(8 * m, 8)], rs.at[ch, e],
-                    rs_send.at[ch, e], rs_recv.at[ch, e], along_col(dy, dw),
-                )
-                copy.start()
-                copies.append(copy)
-        rs_copies.append(copies)
-        if ch == 1:
-            send_x(2)
-
-    mine = rows(8 * (4 * yl + w), 8)
+        for d in (2, 1, 3):
+            if ic == 0:
+                to, part = along_z(d), u.at[ch, :, (w + d) % 4]
+            else:
+                to, part = along_y(d), u.at[ch, (yl + d) % 4]
+            copy = remote(part, ra.at[ch, d - 1], ra_send.at[ch, d - 1], ra_recv.at[ch, d - 1], to)
+            copy.start()
+            copies.append(copy)
+        ra_copies.append(copies)
+    pass_x(1)
+    send_x(2)
+
+    rb_copies = []
+
+    def reduce_first(ch):
+        ic = CHUNKS[ch][1]
+        for copy in ra_copies[ch]:
+            copy.wait_recv()
+        if ic == 0:
+            total = u[ch, :, pl.ds(w, 1)].reshape(4, 8, 512)
+        else:
+            total = u[ch, pl.ds(yl, 1)].reshape(4, 8, 512)
+        sb[ch] = total + ra[ch, 0] + ra[ch, 1] + ra[ch, 2]
+        copies = []
+        for d in (2, 1, 3):
+            to, n = (along_y(d), (yl + d) % 4) if ic == 0 else (along_z(d), (w + d) % 4)
+            copy = remote(sb.at[ch, n], rb.at[ch, d - 1], rb_send.at[ch, d - 1], rb_recv.at[ch, d - 1], to)
+            copy.start()
+            copies.append(copy)
+        rb_copies.append(copies)
+
     slot = (z // 4) * 4 + (z % 2) * 2 + (z // 2) % 2
     slot_rows = rows(8 * slot, 8)
     ag_copies = []
-    relays = []
-    for ch in range(4):
-        for copy in rs_copies[ch]:
+
+    def gather(ch):
+        for copy in rb_copies[ch]:
             copy.wait_recv()
-        total = u[ch, mine]
-        for e in range(1, 16):
-            total = total + rs[ch, e]
-        ag[ch, slot_rows] = total
+        own = yl if CHUNKS[ch][1] == 0 else w
+        total = sb[ch, pl.ds(own, 1)].reshape(8, 512)
+        ag[ch, slot_rows] = total + rb[ch, 0] + rb[ch, 1] + rb[ch, 2]
         copies = []
         for dz in (4, 3, 5, 2, 6, 1, 7):
             to = device(x, yh, k, yl, (z + dz) % 8)
@@ -182,16 +224,26 @@
             copy.start()
             copies.append(copy)
         ag_copies.append(copies)
-        for d in ((), (1, 3), (2,), ())[ch]:
-            x_copies[d].wait_recv()
-            relay = remote(xb.at[d, 0], xb.at[d, 1], x_send.at[4 + d], x_recv.at[4 + d], sibling)
-            relay.start()
-            relays.append(relay)
+
+    reduce_first(0)
+    reduce_first(1)
+    pass_x(2)
+    send_x(3)
+    gather(0)
+    reduce_first(2)
+    gather(1)
+    reduce_first(3)
+    gather(2)
+    gather(3)
+    pass_x(3)
 
     own_x.wait()
     copy_xs.wait_recv()
-    for relay in relays:
-        relay.wait_recv()
+    for sends, receives, copy, relay in x_hops:
+
+        @pl.when(receives)
+        def _(relay=relay):
+            relay.wait_recv()
 
     finals = []
     for tc in range(2):
@@ -200,7 +252,8 @@
                 copy.wait_recv()
         a = [split(ag[2 * tc + ic]) for ic in range(2)]
         for d in range(4):
-            op[tc, d] = dot_nt(a[0], split(xb[d, 0])) + dot_nt(a[1], split(xb[d, 1]))
+            block = xb[pl.ds((yl + d) % 4, 1)].reshape(2, 128, 512)
+            op[tc, d] = dot_nt(a[0], split(block[0])) + dot_nt(a[1], split(block[1]))
             for g in range(2):
                 for q in range(2):
                     n = ((tc * 4 + d) * 2 + g) * 2 + q
@@ -245,9 +298,19 @@
             o_ref[place, pl.ds(128 * half, 128)] = total
 
     copy_ty.wait_send()
-    for copies in t_copies + rs_copies + ag_copies + [relays, list(x_copies.values())]:
+    for copies in t_copies + ra_copies + rb_copies + ag_copies:
         for copy in copies:
             copy.wait_send()
+    for sends, receives, copy, relay in x_hops:
+
+        @pl.when(sends)
+        def _(copy=copy):
+            copy.wait_send()
+
+        @pl.when(receives)
+        def _(relay=relay):
+            relay.wait_send()
+
     for copy in (copy_mp, copy_ms, copy_mr, copy_xs):
         copy.wait_send()
     for here, copy in finals:
@@ -270,22 +333,25 @@
             vmem((4, 2, 128, 512), F32),
             vmem((8, 8, 256), F32),
             vmem((3, 32, 8, 256), F32),
-            vmem((4, 128, 512), F32),
-            vmem((4, 16, 8, 512), F32),
+            vmem((4, 4, 4, 8, 512), F32),
+            vmem((4, 3, 4, 8, 512), F32),
+            vmem((4, 4, 8, 512), F32),
+            vmem((4, 3, 8, 512), F32),
             vmem((4, 64, 512), F32),
             vmem((2, 4, 64, 128), F32),
             vmem((8, 2, 32, 128), F32),
             dma((4,)),
             dma((3,)), dma((3,)),
-            dma((8,)), dma((8,)),
+            dma((13,)), dma((13,)),
             dma, dma,
             dma((24,)), dma((24,)),
-            dma((4, 16)), dma((4, 16)),
+            dma((4, 3)), dma((4, 3)),
+            dma((4, 3)), dma((4, 3)),
             dma((4, 8)), dma((4, 8)),
             dma((32,)), dma((2, 8, 2)),
         ],
         compiler_params=pltpu.CompilerParams(
-            collective_id=0, has_side_effects=True, vmem_limit_bytes=48 * 2**20
+            collective_id=0, has_side_effects=True, vmem_limit_bytes=64 * 2**20 - 2**16
         ),
         cost_estimate=pl.CostEstimate(flops=1207959552, bytes_accessed=2 * 2**20, transcendentals=0),
         name="scores",

time: 94.2 us -> 86.9 us (0.923)
  the two profiles are of different devices: /device:TPU:33 before, /device:TPU:9 now
where the time goes in v3:
time: 86.9 us; the launch traced here: 86.8 us
  Pallas kernels  85.4 us (98%)
  local copies, waits for them, and re-layouts  1.38 us (2%)
    pallas_call x1, Pallas kernels, on_device(): pl.pallas_call(kernel, out_shape=jax.ShapeDtypeStruct((32, 256), F32), in...  85.4 us

profile of v3, /device:TPU:9, one launch (start us, length us, event | category | flops | bytes accessed | tf_op | source)
XLA Modules:
  0.0 86.8 jit_solution(10933647323428728215)
XLA Ops:
  0.0 85.4 %scores.1 = f32[32,256]{1,0:T(8,128)} custom-call(f32[128,512]{1,0:T(8,128)} %x_ref.1, f32[512,256]{1,0:T(8,128)} %m_ref.1, f32[8,8,256]{2,1,0:T(8,128)} %bitcast.1), custom_call_target="tpu_custom_call" | custom-call | flops 1207959552 | bytes 2097152 | tf_op jit(solution)/shard_map/scores/pallas_call | solution.py:326
  85.4 1.4 %copy.5 = f32[32,256]{1,0:T(8,128)} copy(f32[32,256]{1,0:T(8,128)} %scores.1) | data formatting | bytes 65536

commit v4 on v3

--- a/solution.py
+++ b/solution.py
@@ -29,9 +29,9 @@
 
 def kernel(
     x_ref, m_ref, t_ref, o_ref,
-    mb, xb, ty, tb, u, ra, sb, rb, ag, op, fr,
+    mb, xb, ty, tb, u, ra, sb, rb, ag, op, fa, fs, fr,
     local_sem, m_send, m_recv, x_send, x_recv, ty_send, ty_recv, t_send, t_recv,
-    ra_send, ra_recv, rb_send, rb_recv, ag_send, ag_recv, f_send, f_recv,
+    ra_send, ra_recv, rb_send, rb_recv, ag_send, ag_recv, fa_send, fa_recv, f_send, f_recv,
 ):
     r = lax.axis_index("row")
     c = lax.axis_index("col")
@@ -84,35 +84,6 @@
 
     copy_ty = remote(t_ref, ty, ty_send, ty_recv, across)
     copy_ty.start()
-    t_copies = [[], [], []]
-
-    def send_t(block_ref, b):
-        to_rows = rows(4 * (2 * x + (yh if b == 0 else 1 - yh)), 4)
-        for dx in (2, 1, 3, 0):
-            for q in (1, 0, 2):
-                if dx == 0 and q == 0:
-                    continue
-                half = p if q == 0 else 1 - p
-                n = (b * 4 + dx) * 3 + q
-                copy = remote(
-                    block_ref.at[rows(4 * half, 4)], tb.at[q, to_rows],
-                    t_send.at[n], t_recv.at[n], along_x(dx, q),
-                )
-                copy.start()
-                t_copies[q].append(copy)
-
-    send_t(t_ref, 0)
-    copy_mp = remote(m_ref, mb.at[1, 0], m_send.at[0], m_recv.at[0], along_x(0, 1))
-    copy_mp.start()
-    copy_ms = remote(m_ref, mb.at[0, 1], m_send.at[1], m_recv.at[1], sibling)
-    copy_ms.start()
-    copy_ty.wait_recv()
-    send_t(ty, 1)
-    own_ty = pltpu.make_async_copy(
-        ty.at[rows(4 * p, 4)], tb.at[0, rows(4 * (2 * x + 1 - yh), 4)], local_sem.at[3]
-    )
-    own_ty.start()
-
     x_hops = []
 
     def send_x(hop):
@@ -150,6 +121,35 @@
     copy_xs = remote(x_ref, xb.at[yl, 1], x_send.at[6], x_recv.at[6], sibling)
     copy_xs.start()
 
+    t_copies = [[], [], []]
+
+    def send_t(block_ref, b):
+        to_rows = rows(4 * (2 * x + (yh if b == 0 else 1 - yh)), 4)
+        for dx in (2, 1, 3, 0):
+            for q in (1, 0, 2):
+                if dx == 0 and q == 0:
+                    continue
+                half = p if q == 0 else 1 - p
+                n = (b * 4 + dx) * 3 + q
+                copy = remote(
+                    block_ref.at[rows(4 * half, 4)], tb.at[q, to_rows],
+                    t_send.at[n], t_recv.at[n], along_x(dx, q),
+                )
+                copy.start()
+                t_copies[q].append(copy)
+
+    send_t(t_ref, 0)
+    copy_mp = remote(m_ref, mb.at[1, 0], m_send.at[0], m_recv.at[0], along_x(0, 1))
+    copy_mp.start()
+    copy_ms = remote(m_ref, mb.at[0, 1], m_send.at[1], m_recv.at[1], sibling)
+    copy_ms.start()
+    copy_ty.wait_recv()
+    send_t(ty, 1)
+    own_ty = pltpu.make_async_copy(
+        ty.at[rows(4 * p, 4)], tb.at[0, rows(4 * (2 * x + 1 - yh), 4)], local_sem.at[3]
+    )
+    own_ty.start()
+
     own_m.wait()
     own_t.wait()
     own_ty.wait()
@@ -159,6 +159,8 @@
     copy_mr = remote(mb.at[1, 0], mb.at[1, 1], m_send.at[2], m_recv.at[2], sibling)
     copy_mr.start()
 
+    pass_x(1)
+    send_x(2)
     ra_copies = []
     for ch, (tc, ic) in enumerate(CHUNKS):
         if ch == 1:
@@ -174,6 +176,9 @@
             dot_nt(test_rows(0), split(mb[0, ic])) + dot_nt(test_rows(1 + ic), split(mb[1, ic]))
         ).reshape(4, 4, 8, 512)
         copies = []
+        if ch >= 2:
+            for copy in ra_copies[ch - 2]:
+                copy.wait_send()
         for d in (2, 1, 3):
             if ic == 0:
                 to, part = along_z(d), u.at[ch, :, (w + d) % 4]
@@ -183,8 +188,6 @@
             copy.start()
             copies.append(copy)
         ra_copies.append(copies)
-    pass_x(1)
-    send_x(2)
 
     rb_copies = []
 
@@ -246,59 +249,74 @@
             relay.wait_recv()
 
     finals = []
+    fa_copies = []
     for tc in range(2):
         for ch in (2 * tc, 2 * tc + 1):
             for copy in ag_copies[ch]:
                 copy.wait_recv()
         a = [split(ag[2 * tc + ic]) for ic in range(2)]
-        for d in range(4):
-            block = xb[pl.ds((yl + d) % 4, 1)].reshape(2, 128, 512)
-            op[tc, d] = dot_nt(a[0], split(block[0])) + dot_nt(a[1], split(block[1]))
-            for g in range(2):
-                for q in range(2):
-                    n = ((tc * 4 + d) * 2 + g) * 2 + q
-                    to = device((yl + d) % 4, z // 4, (z // 2) % 2, yl, 4 * g + 2 * k + q)
-                    here = jnp.logical_and(to[0] == r, to[1] == c)
-                    tile = pl.ds(16 * (2 * g + q), 16)
-                    place = pl.ds(16 * tc, 16)
-                    copy = remote(
-                        op.at[tc, d, tile], fr.at[rp, z % 2, place],
-                        f_send.at[n], f_recv.at[tc, rp, z % 2], to,
-                    )
-                    finals.append((here, copy))
-
-                    @pl.when(jnp.logical_not(here))
-                    def _(copy=copy):
-                        copy.start()
-
-                    @pl.when(here)
-                    def _(d=d, tile=tile, place=place):
-                        fr[rp, z % 2, place] = op[tc, d, tile]
+        copies = []
+        for dx in (2, 1, 3, 0):
+            block = xb[pl.ds((x + dx) % 4, 1)].reshape(2, 128, 512)
+            op[tc, dx] = dot_nt(a[0], split(block[0])) + dot_nt(a[1], split(block[1]))
+            if dx:
+                copy = remote(
+                    op.at[tc, dx], fa.at[tc, dx - 1],
+                    fa_send.at[tc, dx - 1], fa_recv.at[tc, dx - 1], along_x(dx, 0),
+                )
+                copy.start()
+                copies.append(copy)
+        fa_copies.append(copies)
+
+    core_out = (z // 2) % 2
+    for tc in range(2):
+        for copy in fa_copies[tc]:
+            copy.wait_recv()
+        fs[tc] = op[tc, 0] + fa[tc, 0] + fa[tc, 1] + fa[tc, 2]
+        place = pl.ds(16 * tc, 16)
+        for g in range(2):
+            for q in range(2):
+                n = 2 * g + q
+                z_out = 4 * g + 2 * k + q
+                here = jnp.logical_and(
+                    jnp.logical_and(yh == z // 4, k == core_out), z == z_out
+                )
+                tile = pl.ds(16 * n, 16)
+                copy = remote(
+                    fs.at[tc, tile], fr.at[yh, z % 2, place],
+                    f_send.at[tc, n], f_recv.at[tc, yh, z % 2],
+                    device(x, z // 4, core_out, yl, z_out),
+                )
+                finals.append((here, copy))
+
+                @pl.when(jnp.logical_not(here))
+                def _(copy=copy):
+                    copy.start()
+
+                @pl.when(here)
+                def _(tc=tc, tile=tile, place=place):
+                    fr[yh, z % 2, place] = fs[tc, tile]
 
     for tc in range(2):
         place = pl.ds(16 * tc, 16)
         for half in range(2):
-            for s in range(8):
-                z_from = 4 * yh + 2 * k + half
+            for s in range(2):
                 here = jnp.logical_and(
-                    jnp.logical_and(rp == s, z_from == z), k == (z // 2) % 2
+                    jnp.logical_and(yh == s, 4 * yh + 2 * k + half == z), k == core_out
                 )
                 arrival = remote(
-                    op.at[0, 0, pl.ds(0, 16)], fr.at[s, half, place],
-                    f_send.at[0], f_recv.at[tc, s, half], sibling,
+                    fs.at[0, pl.ds(0, 16)], fr.at[s, half, place],
+                    f_send.at[0, 0], f_recv.at[tc, s, half], sibling,
                 )
 
                 @pl.when(jnp.logical_not(here))
                 def _(arrival=arrival):
                     arrival.wait_recv()
 
-            total = fr[0, half, place]
-            for s in range(1, 8):
-                total = total + fr[s, half, place]
-            o_ref[place, pl.ds(128 * half, 128)] = total
+            o_ref[place, pl.ds(128 * half, 128)] = fr[0, half, place] + fr[1, half, place]
 
     copy_ty.wait_send()
-    for copies in t_copies + ra_copies + rb_copies + ag_copies:
+    for copies in t_copies + ra_copies[2:] + rb_copies + ag_copies + fa_copies:
         for copy in copies:
             copy.wait_send()
     for sends, receives, copy, relay in x_hops:
@@ -339,7 +357,9 @@
             vmem((4, 3, 8, 512), F32),
             vmem((4, 64, 512), F32),
             vmem((2, 4, 64, 128), F32),
-            vmem((8, 2, 32, 128), F32),
+            vmem((2, 3, 64, 128), F32),
+            vmem((2, 64, 128), F32),
+            vmem((2, 2, 32, 128), F32),
             dma((4,)),
             dma((3,)), dma((3,)),
             dma((13,)), dma((13,)),
@@ -348,7 +368,8 @@
             dma((4, 3)), dma((4, 3)),
             dma((4, 3)), dma((4, 3)),
             dma((4, 8)), dma((4, 8)),
-            dma((32,)), dma((2, 8, 2)),
+            dma((2, 3)), dma((2, 3)),
+            dma((2, 4)), dma((2, 2, 2)),
         ],
         compiler_params=pltpu.CompilerParams(
             collective_id=0, has_side_effects=True, vmem_limit_bytes=64 * 2**20 - 2**16

time: 86.9 us -> 79.7 us (0.917)
  the two profiles are of different devices: /device:TPU:9 before, /device:TPU:1 now
where the time goes in v4:
time: 79.7 us; the launch traced here: 79.5 us
  Pallas kernels  78.1 us (98%)
  local copies, waits for them, and re-layouts  1.38 us (2%)
    pallas_call x1, Pallas kernels, on_device(): pl.pallas_call(kernel, out_shape=jax.ShapeDtypeStruct((32, 256), F32), in...  78.1 us

profile of v4, /device:TPU:1, one launch (start us, length us, event | category | flops | bytes accessed | tf_op | source)
XLA Modules:
  0.0 79.5 jit_solution(6605876906492301012)
XLA Ops:
  0.0 78.1 %scores.1 = f32[32,256]{1,0:T(8,128)} custom-call(f32[128,512]{1,0:T(8,128)} %x_ref.1, f32[512,256]{1,0:T(8,128)} %m_ref.1, f32[8,8,256]{2,1,0:T(8,128)} %bitcast.1), custom_call_target="tpu_custom_call" | custom-call | flops 1207959552 | bytes 2097152 | tf_op jit(solution)/shard_map/scores/pallas_call | solution.py:344
  78.1 1.4 %copy.5 = f32[32,256]{1,0:T(8,128)} copy(f32[32,256]{1,0:T(8,128)} %scores.1) | data formatting | bytes 65536

commit v5 on v4

--- a/solution.py
+++ b/solution.py
@@ -8,6 +8,7 @@
 MESH = pl.DeviceIdType.MESH
 F32 = jnp.float32
 BF16 = jnp.bfloat16
+AX = (0, 0, 1, 0)
 CHUNKS = ((0, 0), (0, 1), (1, 0), (1, 1))
 
 
@@ -138,9 +139,9 @@
                 copy.start()
                 t_copies[q].append(copy)
 
-    send_t(t_ref, 0)
     copy_mp = remote(m_ref, mb.at[1, 0], m_send.at[0], m_recv.at[0], along_x(0, 1))
     copy_mp.start()
+    send_t(t_ref, 0)
     copy_ms = remote(m_ref, mb.at[0, 1], m_send.at[1], m_recv.at[1], sibling)
     copy_ms.start()
     copy_ty.wait_recv()
@@ -150,6 +151,8 @@
     )
     own_ty.start()
 
+    pass_x(1)
+    send_x(2)
     own_m.wait()
     own_t.wait()
     own_ty.wait()
@@ -159,8 +162,6 @@
     copy_mr = remote(mb.at[1, 0], mb.at[1, 1], m_send.at[2], m_recv.at[2], sibling)
     copy_mr.start()
 
-    pass_x(1)
-    send_x(2)
     ra_copies = []
     for ch, (tc, ic) in enumerate(CHUNKS):
         if ch == 1:
@@ -176,11 +177,8 @@
             dot_nt(test_rows(0), split(mb[0, ic])) + dot_nt(test_rows(1 + ic), split(mb[1, ic]))
         ).reshape(4, 4, 8, 512)
         copies = []
-        if ch >= 2:
-            for copy in ra_copies[ch - 2]:
-                copy.wait_send()
         for d in (2, 1, 3):
-            if ic == 0:
+            if AX[ch] == 0:
                 to, part = along_z(d), u.at[ch, :, (w + d) % 4]
             else:
                 to, part = along_y(d), u.at[ch, (yl + d) % 4]
@@ -195,14 +193,14 @@
         ic = CHUNKS[ch][1]
         for copy in ra_copies[ch]:
             copy.wait_recv()
-        if ic == 0:
+        if AX[ch] == 0:
             total = u[ch, :, pl.ds(w, 1)].reshape(4, 8, 512)
         else:
             total = u[ch, pl.ds(yl, 1)].reshape(4, 8, 512)
         sb[ch] = total + ra[ch, 0] + ra[ch, 1] + ra[ch, 2]
         copies = []
         for d in (2, 1, 3):
-            to, n = (along_y(d), (yl + d) % 4) if ic == 0 else (along_z(d), (w + d) % 4)
+            to, n = (along_y(d), (yl + d) % 4) if AX[ch] == 0 else (along_z(d), (w + d) % 4)
             copy = remote(sb.at[ch, n], rb.at[ch, d - 1], rb_send.at[ch, d - 1], rb_recv.at[ch, d - 1], to)
             copy.start()
             copies.append(copy)
@@ -215,7 +213,7 @@
     def gather(ch):
         for copy in rb_copies[ch]:
             copy.wait_recv()
-        own = yl if CHUNKS[ch][1] == 0 else w
+        own = yl if AX[ch] == 0 else w
         total = sb[ch, pl.ds(own, 1)].reshape(8, 512)
         ag[ch, slot_rows] = total + rb[ch, 0] + rb[ch, 1] + rb[ch, 2]
         copies = []
@@ -316,7 +314,7 @@
             o_ref[place, pl.ds(128 * half, 128)] = fr[0, half, place] + fr[1, half, place]
 
     copy_ty.wait_send()
-    for copies in t_copies + ra_copies[2:] + rb_copies + ag_copies + fa_copies:
+    for copies in t_copies + ra_copies + rb_copies + ag_copies + fa_copies:
         for copy in copies:
             copy.wait_send()
     for sends, receives, copy, relay in x_hops:

time: 79.7 us -> 78 us (0.979)
  Pallas kernels: 78.1 us -> 76.4 us
    pallas_call x1, Pallas kernels: 78.1 us -> 76.4 us  [on_device(): pl.pallas_call(kernel, out_shape=jax.ShapeDtypeStruct((32, 256), F32), in...]
where the time goes in v5:
time: 78 us; the launch traced here: 77.8 us
  Pallas kernels  76.4 us (98%)
  local copies, waits for them, and re-layouts  1.38 us (2%)
    pallas_call x1, Pallas kernels, on_device(): pl.pallas_call(kernel, out_shape=jax.ShapeDtypeStruct((32, 256), F32), in...  76.4 us

profile of v5, /device:TPU:1, one launch (start us, length us, event | category | flops | bytes accessed | tf_op | source)
XLA Modules:
  0.0 77.8 jit_solution(15713713119932775041)
XLA Ops:
  0.0 76.4 %scores.1 = f32[32,256]{1,0:T(8,128)} custom-call(f32[128,512]{1,0:T(8,128)} %x_ref.1, f32[512,256]{1,0:T(8,128)} %m_ref.1, f32[8,8,256]{2,1,0:T(8,128)} %bitcast.1), custom_call_target="tpu_custom_call" | custom-call | flops 1207959552 | bytes 2097152 | tf_op jit(solution)/shard_map/scores/pallas_call | solution.py:342
  76.4 1.4 %copy.5 = f32[32,256]{1,0:T(8,128)} copy(f32[32,256]{1,0:T(8,128)} %scores.1) | data formatting | bytes 65536

commit v6 on v5

--- a/solution.py
+++ b/solution.py
@@ -30,7 +30,7 @@
 
 def kernel(
     x_ref, m_ref, t_ref, o_ref,
-    mb, xb, ty, tb, u, ra, sb, rb, ag, op, fa, fs, fr,
+    mb, ms, xb, xs, ty, tb, u, ra, sb, rb, ag, op, fa, fs, fr,
     local_sem, m_send, m_recv, x_send, x_recv, ty_send, ty_recv, t_send, t_recv,
     ra_send, ra_recv, rb_send, rb_recv, ag_send, ag_recv, fa_send, fa_recv, f_send, f_recv,
 ):
@@ -153,7 +153,19 @@
 
     pass_x(1)
     send_x(2)
+    made = set()
+
+    def inverse_halves(j, ic):
+        if (j, ic) not in made:
+            made.add((j, ic))
+            ms[0, j, ic], ms[1, j, ic] = split(mb[j, ic])
+        return ms[0, j, ic], ms[1, j, ic]
+
     own_m.wait()
+    inverse_halves(0, 0)
+    copy_ms.wait_recv()
+    inverse_halves(0, 1)
+
     own_t.wait()
     own_ty.wait()
     for copy in t_copies[0] + t_copies[1]:
@@ -167,14 +179,13 @@
         if ch == 1:
             for copy in t_copies[2]:
                 copy.wait_recv()
-            copy_ms.wait_recv()
             copy_mr.wait_recv()
 
         def test_rows(q):
             return split(tb[q].reshape(8, 2, 16, 256)[:, tc].reshape(128, 256))
 
         u[ch] = (
-            dot_nt(test_rows(0), split(mb[0, ic])) + dot_nt(test_rows(1 + ic), split(mb[1, ic]))
+            dot_nt(test_rows(0), inverse_halves(0, ic)) + dot_nt(test_rows(1 + ic), inverse_halves(1, ic))
         ).reshape(4, 4, 8, 512)
         copies = []
         for d in (2, 1, 3):
@@ -255,8 +266,11 @@
         a = [split(ag[2 * tc + ic]) for ic in range(2)]
         copies = []
         for dx in (2, 1, 3, 0):
-            block = xb[pl.ds((x + dx) % 4, 1)].reshape(2, 128, 512)
-            op[tc, dx] = dot_nt(a[0], split(block[0])) + dot_nt(a[1], split(block[1]))
+            if tc == 0:
+                xs[0, dx], xs[1, dx] = split(xb[pl.ds((x + dx) % 4, 1)].reshape(2, 128, 512))
+            op[tc, dx] = dot_nt(a[0], (xs[0, dx, 0], xs[1, dx, 0])) + dot_nt(
+                a[1], (xs[0, dx, 1], xs[1, dx, 1])
+            )
             if dx:
                 copy = remote(
                     op.at[tc, dx], fa.at[tc, dx - 1],
@@ -346,7 +360,9 @@
         out_specs=pl.BlockSpec(memory_space=pltpu.VMEM),
         scratch_shapes=[
             vmem((2, 2, 512, 256), F32),
+            vmem((2, 2, 2, 512, 256), BF16),
             vmem((4, 2, 128, 512), F32),
+            vmem((2, 4, 2, 128, 512), BF16),
             vmem((8, 8, 256), F32),
             vmem((3, 32, 8, 256), F32),
             vmem((4, 4, 4, 8, 512), F32),

time: 78 us -> 77.8 us (level)
  no operation moved by 1% of the time
where the time goes in v6:
time: 77.8 us; the launch traced here: 77.6 us
  Pallas kernels  76.2 us (98%)
  local copies, waits for them, and re-layouts  1.38 us (2%)
    pallas_call x1, Pallas kernels, on_device(): pl.pallas_call(kernel, out_shape=jax.ShapeDtypeStruct((32, 256), F32), in...  76.2 us

profile of v6, /device:TPU:1, one launch (start us, length us, event | category | flops | bytes accessed | tf_op | source)
XLA Modules:
  0.0 77.6 jit_solution(12989137079003673446)
XLA Ops:
  0.0 76.2 %scores.1 = f32[32,256]{1,0:T(8,128)} custom-call(f32[128,512]{1,0:T(8,128)} %x_ref.1, f32[512,256]{1,0:T(8,128)} %m_ref.1, f32[8,8,256]{2,1,0:T(8,128)} %bitcast.1), custom_call_target="tpu_custom_call" | custom-call | flops 1207959552 | bytes 2097152 | tf_op jit(solution)/shard_map/scores/pallas_call | solution.py:356
  76.2 1.4 %copy.5 = f32[32,256]{1,0:T(8,128)} copy(f32[32,256]{1,0:T(8,128)} %scores.1) | data formatting | bytes 65536

commit v7 on v6

--- a/solution.py
+++ b/solution.py
@@ -239,9 +239,9 @@
 
     reduce_first(0)
     reduce_first(1)
+    gather(0)
     pass_x(2)
     send_x(3)
-    gather(0)
     reduce_first(2)
     gather(1)
     reduce_first(3)

time: 77.8 us -> 77.8 us (level)
  no operation moved by 1% of the time
where the time goes in v7:
time: 77.8 us; the launch traced here: 77.6 us
  Pallas kernels  76.2 us (98%)
  local copies, waits for them, and re-layouts  1.38 us (2%)
    pallas_call x1, Pallas kernels, on_device(): pl.pallas_call(kernel, out_shape=jax.ShapeDtypeStruct((32, 256), F32), in...  76.2 us

profile of v7, /device:TPU:1, one launch (start us, length us, event | category | flops | bytes accessed | tf_op | source)
XLA Modules:
  0.0 77.6 jit_solution(2034486413268719486)
XLA Ops:
  0.0 76.2 %scores.1 = f32[32,256]{1,0:T(8,128)} custom-call(f32[128,512]{1,0:T(8,128)} %x_ref.1, f32[512,256]{1,0:T(8,128)} %m_ref.1, f32[8,8,256]{2,1,0:T(8,128)} %bitcast.1), custom_call_target="tpu_custom_call" | custom-call | flops 1207959552 | bytes 2097152 | tf_op jit(solution)/shard_map/scores/pallas_call | solution.py:356
  76.2 1.4 %copy.5 = f32[32,256]{1,0:T(8,128)} copy(f32[32,256]{1,0:T(8,128)} %scores.1) | data formatting | bytes 65536

commit v8 on v6

--- a/solution.py
+++ b/solution.py
@@ -8,7 +8,7 @@
 MESH = pl.DeviceIdType.MESH
 F32 = jnp.float32
 BF16 = jnp.bfloat16
-AX = (0, 0, 1, 0)
+AX = (0, 1, 0, 0)
 CHUNKS = ((0, 0), (0, 1), (1, 0), (1, 1))
 
 

time: 77.8 us -> 77.9 us (level)
  no operation moved by 1% of the time
where the time goes in v8:
time: 77.9 us; the launch traced here: 77.7 us
  Pallas kernels  76.4 us (98%)
  local copies, waits for them, and re-layouts  1.38 us (2%)
    pallas_call x1, Pallas kernels, on_device(): pl.pallas_call(kernel, out_shape=jax.ShapeDtypeStruct((32, 256), F32), in...  76.4 us

profile of v8, /device:TPU:1, one launch (start us, length us, event | category | flops | bytes accessed | tf_op | source)
XLA Modules:
  0.0 77.7 jit_solution(13339620048369640191)
XLA Ops:
  0.0 76.4 %scores.1 = f32[32,256]{1,0:T(8,128)} custom-call(f32[128,512]{1,0:T(8,128)} %x_ref.1, f32[512,256]{1,0:T(8,128)} %m_ref.1, f32[8,8,256]{2,1,0:T(8,128)} %bitcast.1), custom_call_target="tpu_custom_call" | custom-call | flops 1207959552 | bytes 2097152 | tf_op jit(solution)/shard_map/scores/pallas_call | solution.py:356
  76.4 1.4 %copy.5 = f32[32,256]{1,0:T(8,128)} copy(f32[32,256]{1,0:T(8,128)} %scores.1) | data formatting | bytes 65536
